TPU v7x, 128 devices: a whole 4x4x4 slice. The times are simulated.
128 devices in a mesh: fsdp: 16 (over y, z), tp: 8 (over x, core).
Axes of the slice: x: 4, y: 4, z: 4, core: 2. Of those that a mesh axis runs over, the one named last changes fastest.
Arguments:
- tokens: bfloat16 [4096, 4096], P('fsdp', 'tp'), may hold values from -6 to 6
- gate_tiles: bfloat16 [288, 1024, 128], P('fsdp', 'tp'), may hold values from -0.125 to 0.125
- up_tiles: bfloat16 [288, 1024, 128], P('fsdp', 'tp'), may hold values from -0.125 to 0.125
- gate_slots: int32 [288, 8], P(None, 'tp'), may hold values from -1 to 27, as said below
- up_slots: int32 [288, 8], P(None, 'tp'), may hold values from -1 to 27, as said below
- cotangent: bfloat16 [4096, 14336], P('fsdp', 'tp'), may hold values from -6 to 6
Outputs:
- hidden: bfloat16 [4096, 14336], P('fsdp', 'tp')
- input_grad: bfloat16 [4096, 4096], P('fsdp', 'tp')
- gate_tile_grad: bfloat16 [288, 1024, 128], P('fsdp', 'tp')
- up_tile_grad: bfloat16 [288, 1024, 128], P('fsdp', 'tp')
Inputs may be any that keep to these rules, and one draw needn't show every extreme that they name: `gate_slots`: for each owner (rows f * 18 to (f + 1) * 18 - 1, column t) the non-negative entries are distinct positions of that owner, stand before its -1 entries, and number 10 to 18; in every draw some owner fills all 18 slots. `up_slots`: as for gate_slots, drawn independently.
All inputs are finite; a program needn't handle non-finite values.
Results may differ from a plain program's by a relative error of at most 0.02.
Values may be sent and summed in bfloat16 or wider, within the bound.
No kernel may reach another device: no remote copies, remote signals or barrier semaphores. Data moves between devices by JAX's collectives and lax.ppermute only.
A program may use at most 192 MiB of HBM per device.

v0:
```python
import jax
import jax.numpy as jnp
from jax import lax
from jax.sharding import PartitionSpec as P


def per_device(tokens, gate_tiles, up_tiles, gate_slots, up_slots, cotangent):
    n_fsdp = lax.axis_size("fsdp")
    n_tp = lax.axis_size("tp")
    tile_size = gate_tiles.shape[-1]
    capacity = gate_tiles.shape[0]
    tok_rows = tokens.shape[0]
    gathered = lax.all_gather(tokens, "tp", axis=1, tiled=True)
    model_width = gathered.shape[1]
    ff_local = cotangent.shape[1]
    row_tiles = model_width // (tile_size * n_fsdp)
    col_tiles = ff_local // tile_size
    owner_tiles = row_tiles * col_tiles
    positions = jnp.arange(owner_tiles, dtype=jnp.int32)
    gate_table = gate_slots.reshape(n_fsdp, capacity)
    up_table = up_slots.reshape(n_fsdp, capacity)

    def selector(table, kind):
        picks = (table[:, :, None] == positions).astype(kind)
        return picks.reshape(table.shape[0], table.shape[1], row_tiles, col_tiles)

    gate_select = selector(gate_table, jnp.bfloat16)
    up_select = selector(up_table, jnp.bfloat16)
    gate_all, up_all = (
        lax.all_gather(gate_tiles, "fsdp", axis=0, tiled=True),
        lax.all_gather(up_tiles, "fsdp", axis=0, tiled=True),
    )

    def unpack(blocks, select):
        dense_tiles = jnp.einsum(
            "fcrj,fcab->frjab",
            select,
            blocks.reshape(n_fsdp, capacity, tile_size, tile_size),
            preferred_element_type=jnp.float32,
        )
        return dense_tiles.astype(jnp.bfloat16)

    w_gate = unpack(gate_all, gate_select)
    w_up = unpack(up_all, up_select)
    token_view = gathered.reshape(tok_rows, n_fsdp, row_tiles, tile_size)
    gate = jnp.einsum(
        "tfra,frjab->tjb", token_view, w_gate, preferred_element_type=jnp.float32
    ).reshape(tok_rows, ff_local)
    up = jnp.einsum(
        "tfra,frjab->tjb", token_view, w_up, preferred_element_type=jnp.float32
    ).reshape(tok_rows, ff_local)
    sigmoid_gate = jax.nn.sigmoid(gate)
    activated = gate * sigmoid_gate
    hidden = (activated * up).astype(jnp.bfloat16)
    upstream = cotangent.astype(jnp.float32)
    gate_grad = (upstream * up * sigmoid_gate * (1.0 + gate * (1.0 - sigmoid_gate))).astype(
        jnp.bfloat16
    )
    up_grad = (upstream * activated).astype(jnp.bfloat16)
    gate_view = gate_grad.reshape(tok_rows, col_tiles, tile_size)
    up_view = up_grad.reshape(tok_rows, col_tiles, tile_size)
    total = jnp.einsum(
        "frjab,tjb->frat", w_gate, gate_view, preferred_element_type=jnp.float32
    ) + jnp.einsum("frjab,tjb->frat", w_up, up_view, preferred_element_type=jnp.float32)
    input_part = lax.psum_scatter(
        total.reshape(model_width // n_tp * lax.axis_size("tp"), tok_rows).astype(jnp.bfloat16),
        "tp",
        scatter_dimension=0,
        tiled=True,
    ).astype(jnp.float32)
    input_grad = input_part.T.astype(jnp.bfloat16)
    gate_dense = jnp.einsum(
        "tfra,tjb->frajb", token_view, gate_view, preferred_element_type=jnp.float32
    ).astype(jnp.bfloat16)
    up_dense = jnp.einsum(
        "tfra,tjb->frajb", token_view, up_view, preferred_element_type=jnp.float32
    ).astype(jnp.bfloat16)
    gate_packed = jnp.einsum(
        "fcrj,frajb->fcab", gate_select, gate_dense, preferred_element_type=jnp.float32
    )
    up_packed = jnp.einsum(
        "fcrj,frajb->fcab", up_select, up_dense, preferred_element_type=jnp.float32
    )
    gate_packed = gate_packed.reshape(capacity * lax.axis_size("fsdp"), tile_size, tile_size)
    up_packed = up_packed.reshape(capacity * lax.axis_size("fsdp"), tile_size, tile_size)
    summed = lax.psum_scatter(
        jnp.concatenate([gate_packed, up_packed], axis=2).astype(jnp.bfloat16),
        "fsdp",
        scatter_dimension=0,
        tiled=True,
    ).astype(jnp.float32)
    gate_tile_grad = summed[:, :, :tile_size].astype(jnp.bfloat16)
    up_tile_grad = summed[:, :, tile_size:].astype(jnp.bfloat16)
    return (hidden, input_grad, gate_tile_grad, up_tile_grad)


def solution(mesh):
    placed = (
        P("fsdp", "tp"),
        P("fsdp", "tp", None),
        P("fsdp", "tp", None),
        P(None, "tp"),
        P(None, "tp"),
        P("fsdp", "tp"),
    )
    return jax.shard_map(
        per_device,
        mesh=mesh,
        in_specs=placed,
        out_specs=(P("fsdp", "tp"), P("fsdp", "tp"), P("fsdp", "tp", None), P("fsdp", "tp", None)),
        check_vma=False,
    )
```

profile of v0, /device:TPU:0, one launch (start us, length us, event | category | flops | bytes accessed | tf_op | source)
XLA Modules:
  0.0 513.8 jit_solution(2433849524178457601)
XLA Ops:
  12.1 2.2 copy.67
  14.3 74.0 %all-gather.4.cloned.1.call-done = bf16[288,128,128]{2,1,0:T(8,128)(2,1)} async-done(((bf16[18,128,128]{2,1,0:T(8,128)(2,1)}), bf16[288,128,128]{2,1,0:T(8,128)(2,1)}) %all-gather.4.cloned.1.call-update) | async-done | bytes 9437200 | tf_op jit(solution)/shard_map/all_gather | solution.py:30
  88.4 16.0 %fusion.2 = bf16[16,2,14,128,128]{4,2,3,1,0:T(8,128)(2,1)} fusion(bf16[16,18,128,128,1]{3,2,1,0,4:T(8,128)(2,1)} %bitcast.119, s32[2,14]{1,0:T(2,128)S(1)} %multiply_add_fusion, s32[16,18]{1,0:T(8,128)S(1)} %eq.42), kind=kOutput, calls=%fused_computation.9 | convolution fusion | flops 264249216 | bytes 24118512 | tf_op jit(solution)/shard_map/fcrj,fcab->frjab/dot_general | solution.py:35
  104.4 11.0 %all-gather.6.cloned.1.call-done = bf16[256,4096]{0,1:T(8,128)(2,1)} async-done(((bf16[256,512]{0,1:T(8,128)(2,1)}), bf16[256,4096]{0,1:T(8,128)(2,1)}) %all-gather.6.cloned.1.call-update) | async-done | bytes 2097168 | tf_op jit(solution)/shard_map/all_gather | solution.py:13
  115.4 14.4 %fusion.6 = f32[14,128,256,1,1]{2,1,0,4,3:T(8,128)} fusion(bf16[256,16,2,128,1]{0,3,4,2,1:T(8,128)(2,1)} %bitcast.121, bf16[16,2,14,128,128]{4,2,3,1,0:T(8,128)(2,1)} %fusion.2), kind=kOutput, calls=%fused_computation.14 | convolution fusion | flops 3758096384 | bytes 18612224 | tf_op jit(solution)/shard_map/tfra,frjab->tjb/dot_general | solution.py:46
  129.8 63.8 %all-gather.8.cloned.1.call-done = bf16[288,128,128]{2,1,0:T(8,128)(2,1)} async-done(((bf16[18,128,128]{2,1,0:T(8,128)(2,1)}), bf16[288,128,128]{2,1,0:T(8,128)(2,1)}) %all-gather.8.cloned.1.call-update) | async-done | bytes 9437200 | tf_op jit(solution)/shard_map/all_gather | solution.py:31
  193.6 15.7 %fusion = bf16[16,2,14,128,128]{4,2,3,1,0:T(8,128)(2,1)} fusion(bf16[16,18,128,128,1]{3,2,1,0,4:T(8,128)(2,1)} %bitcast.120, s32[16,18]{1,0:T(8,128)S(1)} %eq.49, s32[2,14]{1,0:T(2,128)S(1)} %multiply_add_fusion), kind=kOutput, calls=%fused_computation.7 | convolution fusion | flops 264249216 | bytes 24118512 | tf_op jit(solution)/shard_map/fcrj,fcab->frjab/dot_general | solution.py:35
  209.4 13.6 %fusion.8 = f32[14,128,256,1,1]{2,1,0,4,3:T(8,128)S(1)} fusion(bf16[256,16,2,128,1]{0,3,4,2,1:T(8,128)(2,1)S(1)} %bitcast.122, bf16[16,2,14,128,128]{4,2,3,1,0:T(8,128)(2,1)} %fusion), kind=kOutput, calls=%fused_computation.16 | convolution fusion | flops 3758096384 | bytes 18612224 | tf_op jit(solution)/shard_map/tfra,frjab->tjb/dot_general | solution.py:49
  223.0 2.4 fusion.11
  225.3 7.2 %convert_bitcast_fusion = bf16[16,2,128,14,128]{2,4,1,0,3:T(8,128)(2,1)} fusion(bf16[256,14,128,1,1]{0,2,4,3,1:T(8,128)(2,1)S(1)} %bitcast.125, bf16[256,16,2,128,1]{0,3,2,1,4:T(8,128)(2,1)S(1)} %bitcast.123), kind=kOutput, calls=%fused_computation.5 | convolution fusion | flops 3765436416 | bytes 17694720 | tf_op jit(solution)/shard_map/tfra,tjb->frajb/dot_general | solution.py:75
  232.5 24.7 %copy.75 = bf16[16,2,128,14,128]{4,3,1,2,0:T(8,128)(2,1)} copy(bf16[16,2,128,14,128]{2,4,1,0,3:T(8,128)(2,1)} %convert_bitcast_fusion) | data formatting | bytes 29360128 | tf_op jit(solution)/shard_map/convert_element_type | solution.py:77
  257.2 10.2 %bitcast_convert_fusion = bf16[16,18,128,128]{3,1,2,0:T(8,128)(2,1)} fusion(bf16[16,2,128,14,128]{4,3,1,2,0:T(8,128)(2,1)} %copy.75, s32[16,18]{1,0:T(8,128)S(1)} %eq.49, s32[2,14]{1,0:T(2,128)S(1)} %multiply_add_fusion), kind=kOutput, calls=%fused_computation.2 | convolution fusion | flops 268967808 | bytes 24118512 | tf_op jit(solution)/shard_map/fcrj,frajb->fcab/dot_general | solution.py:81
  267.5 11.0 %copy.76 = bf16[16,18,128,128]{3,2,1,0:T(8,128)(2,1)} copy(bf16[16,18,128,128]{3,1,2,0:T(8,128)(2,1)} %bitcast_convert_fusion) | data formatting | bytes 18874368 | tf_op jit(solution)/shard_map/convert.4
  278.4 8.6 %convert_bitcast_fusion.1 = bf16[16,2,128,14,128]{2,4,1,0,3:T(8,128)(2,1)} fusion(bf16[256,14,128,1,1]{0,2,4,3,1:T(8,128)(2,1)} %bitcast.127, bf16[256,16,2,128,1]{0,3,2,1,4:T(8,128)(2,1)S(1)} %bitcast.124), kind=kOutput, calls=%fused_computation.6 | convolution fusion | flops 3765436416 | bytes 17694720 | tf_op jit(solution)/shard_map/tfra,tjb->frajb/dot_general | solution.py:72
  287.1 24.7 %copy.72 = bf16[16,2,128,14,128]{4,3,1,2,0:T(8,128)(2,1)} copy(bf16[16,2,128,14,128]{2,4,1,0,3:T(8,128)(2,1)} %convert_bitcast_fusion.1) | data formatting | bytes 29360128 | tf_op jit(solution)/shard_map/convert_element_type | solution.py:74
  311.8 10.4 %bitcast_convert_fusion.1 = bf16[16,18,128,128]{3,1,2,0:T(8,128)(2,1)} fusion(bf16[16,2,128,14,128]{4,3,1,2,0:T(8,128)(2,1)} %copy.72, s32[2,14]{1,0:T(2,128)S(1)} %multiply_add_fusion, s32[16,18]{1,0:T(8,128)S(1)} %eq.42), kind=kOutput, calls=%fused_computation.3 | convolution fusion | flops 268967808 | bytes 24118512 | tf_op jit(solution)/shard_map/fcrj,frajb->fcab/dot_general | solution.py:78
  322.2 11.0 %copy.73 = bf16[16,18,128,128]{3,2,1,0:T(8,128)(2,1)} copy(bf16[16,18,128,128]{3,1,2,0:T(8,128)(2,1)} %bitcast_convert_fusion.1) | data formatting | bytes 18874368 | tf_op jit(solution)/shard_map/convert.5
  333.2 16.8 %pad_maximum_fusion = bf16[288,128,256]{2,1,0:T(8,128)(2,1)} fusion(bf16[288,128,128]{2,1,0:T(8,128)(2,1)} %bitcast.117, bf16[288,128,128]{2,1,0:T(8,128)(2,1)} %bitcast.118), kind=kLoop, calls=%fused_computation.4 | loop fusion | flops 37748736 | bytes 37748736 | tf_op jit(solution)/shard_map/concatenate | solution.py:87
  351.2 9.3 %fusion.5 = f32[16,2,128,256,1]{3,2,4,1,0:T(8,128)S(1)} fusion(bf16[256,14,128,1,1]{0,2,1,4,3:T(8,128)(2,1)S(1)} %bitcast.128, bf16[16,2,14,128,128]{4,2,3,1,0:T(8,128)(2,1)} %fusion.2), kind=kOutput, calls=%fused_computation.13 | convolution fusion | flops 3758096384 | bytes 19791872 | tf_op jit(solution)/shard_map/frjab,tjb->frat/dot_general | solution.py:62
  360.5 10.7 %fusion.4 = bf16[16,2,128,256]{3,2,1,0:T(8,128)(2,1)} fusion(f32[16,2,128,256,1]{3,2,4,1,0:T(8,128)S(1)} %fusion.5, bf16[256,14,128,1,1]{0,2,1,4,3:T(8,128)(2,1)S(1)} %bitcast.126, bf16[16,2,14,128,128]{4,2,3,1,0:T(8,128)(2,1)} %fusion), kind=kOutput, calls=%fused_computation.12 | convolution fusion | flops 3760193536 | bytes 21889024 | tf_op jit(solution)/shard_map/frjab,tjb->frat/dot_general | solution.py:64
  371.2 4.1 copy.70
  376.7 94.2 %reduce-scatter.5.cloned.1.call-done = bf16[18,128,256]{2,1,0:T(8,128)(2,1)} async-done(((bf16[288,128,256]{2,1,0:T(8,128)(2,1)}), bf16[18,128,256]{2,1,0:T(8,128)(2,1)}) %reduce-scatter.5.cloned.1.call-update) | async-done | bytes 1179664 | tf_op jit(solution)/shard_map/reduce_scatter | solution.py:86
  470.9 2.4 fusion.26
  473.3 33.8 %reduce-scatter.3.cloned.1.call-done = bf16[512,256]{0,1:T(8,128)(2,1)} async-done(((bf16[4096,256]{0,1:T(8,128)(2,1)}), bf16[512,256]{0,1:T(8,128)(2,1)}) %reduce-scatter.3.cloned.1.call-update) | async-done | bytes 262160 | tf_op jit(solution)/shard_map/reduce_scatter | solution.py:65
  (27 shorter events, 7.5 us)
Async XLA Ops:
  7.2 81.2 %all-gather.4.cloned.1.call-start = ((), (), s32[]{:S(2)}) async-start(), calls=%async_computation.2 | async-start | bytes 10027008 | tf_op jit(solution)/shard_map/all_gather | solution.py:30
  7.9 107.5 %all-gather.6.cloned.1.call-start = ((), (), s32[]{:S(2)}) async-start(), calls=%async_computation.3 | async-start | bytes 2359296 | tf_op jit(solution)/shard_map/all_gather | solution.py:13
  9.8 183.9 %all-gather.8.cloned.1.call-start = ((), (), s32[]{:S(2)}) async-start(), calls=%async_computation.4 | async-start | bytes 10027008 | tf_op jit(solution)/shard_map/all_gather | solution.py:31
  10.5 460.4 %reduce-scatter.5.cloned.1.call-start = ((), (), s32[]{:S(2)}) async-start(), calls=%async_computation.6 | async-start | bytes 20054016 | tf_op jit(solution)/shard_map/reduce_scatter | solution.py:86
  193.6 15.7 %copy-start = (bf16[256,4096]{0,1:T(8,128)(2,1)S(1)}, bf16[256,4096]{0,1:T(8,128)(2,1)}, u32[]{:S(2)}) copy-start(bf16[256,4096]{0,1:T(8,128)(2,1)} %all-gather.6.cloned.1.call-done) | copy-start | bytes 6291460
  209.4 13.6 %copy-start.3 = (bf16[256,1792]{0,1:T(8,128)(2,1)S(1)}, bf16[256,1792]{0,1:T(8,128)(2,1)}, u32[]{:S(2)}) copy-start(bf16[256,1792]{0,1:T(8,128)(2,1)} %copy.67) | copy-start | bytes 2752516
  209.4 13.6 %copy-start.4 = (f32[14,128,256,1,1]{2,1,0,4,3:T(8,128)S(1)}, f32[14,128,256,1,1]{2,1,0,4,3:T(8,128)}, u32[]{:S(2)}) copy-start(f32[14,128,256,1,1]{2,1,0,4,3:T(8,128)} %fusion.6) | copy-start | bytes 5505028
  350.0 1.2 copy-start.1
  350.0 157.1 %reduce-scatter.3.cloned.1.call-start = ((), (), s32[]{:S(2)}) async-start(), calls=%async_computation.5 | async-start | bytes 2359296 | tf_op jit(solution)/shard_map/reduce_scatter | solution.py:65
  360.5 14.9 %copy-start.2 = (bf16[256,1792]{0,1:T(8,128)(2,1)S(1)}, bf16[256,1792]{0,1:T(8,128)(2,1)}, u32[]{:S(2)}) copy-start(bf16[256,1792]{0,1:T(8,128)(2,1)} %get-tuple-element.17) | copy-start | bytes 2752516
Sparse Core Ops, SparseCore 0:
  10.2 78.1 all-gather.3
  90.7 24.6 all-gather.5
  117.6 75.9 all-gather.7
  350.1 120.7 reduce-scatter.4
  473.8 33.2 reduce-scatter.2
where the time goes:
time: 520 us; the launch traced here: 514 us
  waiting for transfers between devices  278 us (53%)
  matrix products  116 us (22%)
  local copies, waits for them, and re-layouts  84.6 us (16%)
  other arithmetic  20.6 us (4%)
  between operations  14.1 us (3%)
    reduce_scatter x1, waiting for transfers between devices, per_device(): lax.psum_scatter(jnp.concatenate([gate_packed, up_packed], axis=2).astype...  94.2 us
    all_gather x1, waiting for transfers between devices, per_device(): lax.all_gather(gate_tiles, 'fsdp', axis=0, tiled=True)  74 us
    all_gather x1, waiting for transfers between devices, per_device(): lax.all_gather(up_tiles, 'fsdp', axis=0, tiled=True)  63.8 us
    reduce_scatter x1, waiting for transfers between devices, per_device(): lax.psum_scatter(total.reshape(model_width // n_tp * lax.axis_size('tp'),...  33.8 us
    dot_general x2, matrix products, unpack(): jnp.einsum('fcrj,fcab->frjab', select, blocks.reshape(n_fsdp, capacity, t...  31.8 us
    convert_element_type x1, local copies, waits for them, and re-layouts, per_device(): up_dense = jnp.einsum('tfra,tjb->frajb', token_view, up_view, preferred_e...  24.7 us
    convert_element_type x1, local copies, waits for them, and re-layouts, per_device(): gate_dense = jnp.einsum('tfra,tjb->frajb', token_view, gate_view, preferr...  24.7 us
    another operation x2, local copies, waits for them, and re-layouts  21.9 us
  transfers between devices with their start and end apart: 5, of which 5 were waited for; matrix products, arithmetic and copies ran while one was open for 12% of the time, Pallas kernels for 0%

commit v1 on v0

--- a/solution.py
+++ b/solution.py
@@ -27,7 +27,9 @@
     gate_select = selector(gate_table, jnp.bfloat16)
     up_select = selector(up_table, jnp.bfloat16)
     gate_all, up_all = (
-        lax.all_gather(gate_tiles, "fsdp", axis=0, tiled=True),
+        jnp.concatenate(
+            lax.all_to_all(jnp.stack([gate_tiles] * lax.axis_size("fsdp")), "fsdp", 0, 0), axis=0
+        ),
         lax.all_gather(up_tiles, "fsdp", axis=0, tiled=True),
     )
 

time: 520 us -> 557 us (1.071)
  waiting for transfers between devices: 278 us -> 300 us
  starting transfers between devices: 0.2 us -> 8.47 us
  local copies, waits for them, and re-layouts: 84.6 us -> 90.7 us
    all_to_all x0 -> x1, waiting for transfers between devices: none -> 151 us  [per_device(): lax.all_to_all(jnp.stack([gate_tiles] * lax.axis_size('fsdp')), 'fsdp', 0...]
    all_gather x1 -> x0, waiting for transfers between devices: 74 us -> none  [per_device(): lax.all_gather(gate_tiles, 'fsdp', axis=0, tiled=True)]
    all_gather x1, waiting for transfers between devices: 63.8 us -> 15.8 us  [per_device(): lax.all_gather(up_tiles, 'fsdp', axis=0, tiled=True)]
    all_gather x1, waiting for transfers between devices: 11 us -> 0.02 us  [per_device(): gathered = lax.all_gather(tokens, 'tp', axis=1, tiled=True)]
    all_to_all x0 -> x1, starting transfers between devices: none -> 8.31 us  [per_device(): lax.all_to_all(jnp.stack([gate_tiles] * lax.axis_size('fsdp')), 'fsdp', 0...]
    another operation x2 -> x3, local copies, waits for them, and re-layouts: 21.9 us -> 29 us
  transfers between devices with their start and end apart: 5 -> 5, of which waited for: 5 -> 4; matrix products, arithmetic and copies ran while one was open for 12% -> 12% of each run, Pallas kernels for 0% -> 0%
where the time goes in v1:
time: 557 us; the launch traced here: 549 us
  waiting for transfers between devices  300 us (54%)
  matrix products  117 us (21%)
  local copies, waits for them, and re-layouts  90.7 us (16%)
  other arithmetic  19.2 us (3%)
  between operations  14.1 us (3%)
  starting transfers between devices  8.47 us (2%)
    all_to_all x1, waiting for transfers between devices, per_device(): lax.all_to_all(jnp.stack([gate_tiles] * lax.axis_size('fsdp')), 'fsdp', 0...  151 us
    reduce_scatter x1, waiting for transfers between devices, per_device(): lax.psum_scatter(jnp.concatenate([gate_packed, up_packed], axis=2).astype...  99 us
    reduce_scatter x1, waiting for transfers between devices, per_device(): lax.psum_scatter(total.reshape(model_width // n_tp * lax.axis_size('tp'),...  33.7 us
    dot_general x2, matrix products, unpack(): jnp.einsum('fcrj,fcab->frjab', select, blocks.reshape(n_fsdp, capacity, t...  31.8 us
    convert_element_type x1, local copies, waits for them, and re-layouts, per_device(): gate_dense = jnp.einsum('tfra,tjb->frajb', token_view, gate_view, preferr...  24.7 us
    convert_element_type x1, local copies, waits for them, and re-layouts, per_device(): up_dense = jnp.einsum('tfra,tjb->frajb', token_view, up_view, preferred_e...  24.7 us
    another operation x2, local copies, waits for them, and re-layouts  21.9 us
    concatenate x1, other arithmetic, per_device(): jnp.concatenate([gate_packed, up_packed], axis=2).astype(jnp.bfloat16)  16.8 us
  transfers between devices with their start and end apart: 5, of which 4 were waited for; matrix products, arithmetic and copies ran while one was open for 12% of the time, Pallas kernels for 0%

profile of v1, /device:TPU:0, one launch (start us, length us, event | category | flops | bytes accessed | tf_op | source)
XLA Modules:
  0.0 549.4 jit_solution(1958983056945469043)
XLA Ops:
  9.8 7.1 %stack.2 = bf16[16,18,128,128]{3,2,1,0:T(8,128)(2,1)} broadcast(bf16[18,128,128]{2,1,0:T(8,128)(2,1)} %param.7), dimensions={1,2,3} | broadcast | bytes 10027008 | tf_op jit(solution)/shard_map/stack | solution.py:31
  16.9 8.3 %all-to-all-start = ((bf16[16,18,128,128]{3,2,1,0:T(8,128)(2,1)}), bf16[16,18,128,128]{3,2,1,0:T(8,128)(2,1)}, u32[]{:S(2)}, u32[]{:S(2)}) async-start(bf16[16,18,128,128]{3,2,1,0:T(8,128)(2,1)} %stack.2), calls=%async_computation | async-start | bytes 18874368 | tf_op jit(solution)/shard_map/all_to_all | solution.py:31
  26.8 150.8 %all-to-all-done = bf16[16,18,128,128]{3,2,1,0:T(8,128)(2,1)} async-done(((bf16[16,18,128,128]{3,2,1,0:T(8,128)(2,1)}), bf16[16,18,128,128]{3,2,1,0:T(8,128)(2,1)}, u32[]{:S(2)}, u32[]{:S(2)}) %all-to-all-start) | async-done | bytes 9437216 | tf_op jit(solution)/shard_map/all_to_all | solution.py:31
  177.7 16.0 %fusion.2 = bf16[16,2,14,128,128]{4,2,3,1,0:T(8,128)(2,1)} fusion(bf16[16,18,128,128,1]{3,2,1,0,4:T(8,128)(2,1)} %bitcast.2, s32[2,14]{1,0:T(2,128)S(1)} %multiply_add_fusion, s32[16,18]{1,0:T(8,128)S(1)} %eq.42), kind=kOutput, calls=%fused_computation.9 | convolution fusion | flops 264249216 | bytes 24118512 | tf_op jit(solution)/shard_map/fcrj,fcab->frjab/dot_general | solution.py:37
  193.7 14.7 %fusion.6 = f32[14,128,256,1,1]{2,1,0,4,3:T(8,128)} fusion(bf16[256,16,2,128,1]{0,3,4,2,1:T(8,128)(2,1)} %bitcast.118, bf16[16,2,14,128,128]{4,2,3,1,0:T(8,128)(2,1)} %fusion.2), kind=kOutput, calls=%fused_computation.14 | convolution fusion | flops 3758096384 | bytes 18612224 | tf_op jit(solution)/shard_map/tfra,frjab->tjb/dot_general | solution.py:48
  208.4 15.8 %all-gather.5.cloned.1.call-done = bf16[288,128,128]{2,1,0:T(8,128)(2,1)} async-done(((bf16[18,128,128]{2,1,0:T(8,128)(2,1)}), bf16[288,128,128]{2,1,0:T(8,128)(2,1)}) %all-gather.5.cloned.1.call-update) | async-done | bytes 9437200 | tf_op jit(solution)/shard_map/all_gather | solution.py:33
  224.3 15.7 %fusion = bf16[16,2,14,128,128]{4,2,3,1,0:T(8,128)(2,1)} fusion(bf16[16,18,128,128,1]{3,2,1,0,4:T(8,128)(2,1)} %bitcast.117, s32[16,18]{1,0:T(8,128)S(1)} %eq.49, s32[2,14]{1,0:T(2,128)S(1)} %multiply_add_fusion), kind=kOutput, calls=%fused_computation.7 | convolution fusion | flops 264249216 | bytes 24118512 | tf_op jit(solution)/shard_map/fcrj,fcab->frjab/dot_general | solution.py:37
  240.0 13.6 %fusion.8 = f32[14,128,256,1,1]{2,1,0,4,3:T(8,128)S(1)} fusion(bf16[256,16,2,128,1]{0,3,4,2,1:T(8,128)(2,1)S(1)} %bitcast.119, bf16[16,2,14,128,128]{4,2,3,1,0:T(8,128)(2,1)} %fusion), kind=kOutput, calls=%fused_computation.16 | convolution fusion | flops 3758096384 | bytes 18612224 | tf_op jit(solution)/shard_map/tfra,frjab->tjb/dot_general | solution.py:51
  253.6 2.4 fusion.11
  256.0 7.2 %convert_bitcast_fusion = bf16[16,2,128,14,128]{2,4,1,0,3:T(8,128)(2,1)} fusion(bf16[256,14,128,1,1]{0,2,4,3,1:T(8,128)(2,1)S(1)} %bitcast.122, bf16[256,16,2,128,1]{0,3,2,1,4:T(8,128)(2,1)S(1)} %bitcast.120), kind=kOutput, calls=%fused_computation.5 | convolution fusion | flops 3765436416 | bytes 17694720 | tf_op jit(solution)/shard_map/tfra,tjb->frajb/dot_general | solution.py:77
  263.2 24.7 %copy.76 = bf16[16,2,128,14,128]{4,3,1,2,0:T(8,128)(2,1)} copy(bf16[16,2,128,14,128]{2,4,1,0,3:T(8,128)(2,1)} %convert_bitcast_fusion) | data formatting | bytes 29360128 | tf_op jit(solution)/shard_map/convert_element_type | solution.py:79
  287.9 10.3 %bitcast_convert_fusion = bf16[16,18,128,128]{3,1,2,0:T(8,128)(2,1)} fusion(bf16[16,2,128,14,128]{4,3,1,2,0:T(8,128)(2,1)} %copy.76, s32[16,18]{1,0:T(8,128)S(1)} %eq.49, s32[2,14]{1,0:T(2,128)S(1)} %multiply_add_fusion), kind=kOutput, calls=%fused_computation.2 | convolution fusion | flops 268967808 | bytes 24118512 | tf_op jit(solution)/shard_map/fcrj,frajb->fcab/dot_general | solution.py:83
  298.2 10.9 %copy.77 = bf16[16,18,128,128]{3,2,1,0:T(8,128)(2,1)} copy(bf16[16,18,128,128]{3,1,2,0:T(8,128)(2,1)} %bitcast_convert_fusion) | data formatting | bytes 18874368 | tf_op jit(solution)/shard_map/convert.4
  309.1 8.6 %convert_bitcast_fusion.1 = bf16[16,2,128,14,128]{2,4,1,0,3:T(8,128)(2,1)} fusion(bf16[256,14,128,1,1]{0,2,4,3,1:T(8,128)(2,1)} %bitcast.124, bf16[256,16,2,128,1]{0,3,2,1,4:T(8,128)(2,1)S(1)} %bitcast.121), kind=kOutput, calls=%fused_computation.6 | convolution fusion | flops 3765436416 | bytes 17694720 | tf_op jit(solution)/shard_map/tfra,tjb->frajb/dot_general | solution.py:74
  317.8 24.7 %copy.73 = bf16[16,2,128,14,128]{4,3,1,2,0:T(8,128)(2,1)} copy(bf16[16,2,128,14,128]{2,4,1,0,3:T(8,128)(2,1)} %convert_bitcast_fusion.1) | data formatting | bytes 29360128 | tf_op jit(solution)/shard_map/convert_element_type | solution.py:76
  342.5 10.4 %bitcast_convert_fusion.1 = bf16[16,18,128,128]{3,1,2,0:T(8,128)(2,1)} fusion(bf16[16,2,128,14,128]{4,3,1,2,0:T(8,128)(2,1)} %copy.73, s32[2,14]{1,0:T(2,128)S(1)} %multiply_add_fusion, s32[16,18]{1,0:T(8,128)S(1)} %eq.42), kind=kOutput, calls=%fused_computation.3 | convolution fusion | flops 268967808 | bytes 24118512 | tf_op jit(solution)/shard_map/fcrj,frajb->fcab/dot_general | solution.py:80
  352.9 11.0 %copy.74 = bf16[16,18,128,128]{3,2,1,0:T(8,128)(2,1)} copy(bf16[16,18,128,128]{3,1,2,0:T(8,128)(2,1)} %bitcast_convert_fusion.1) | data formatting | bytes 18874368 | tf_op jit(solution)/shard_map/convert.5
  363.9 16.8 %pad_maximum_fusion = bf16[288,128,256]{2,1,0:T(8,128)(2,1)} fusion(bf16[288,128,128]{2,1,0:T(8,128)(2,1)} %bitcast.115, bf16[288,128,128]{2,1,0:T(8,128)(2,1)} %bitcast.116), kind=kLoop, calls=%fused_computation.4 | loop fusion | flops 37748736 | bytes 37748736 | tf_op jit(solution)/shard_map/concatenate | solution.py:89
  381.8 9.3 %fusion.5 = f32[16,2,128,256,1]{3,2,4,1,0:T(8,128)S(1)} fusion(bf16[256,14,128,1,1]{0,2,1,4,3:T(8,128)(2,1)S(1)} %bitcast.125, bf16[16,2,14,128,128]{4,2,3,1,0:T(8,128)(2,1)} %fusion.2), kind=kOutput, calls=%fused_computation.13 | convolution fusion | flops 3758096384 | bytes 19791872 | tf_op jit(solution)/shard_map/frjab,tjb->frat/dot_general | solution.py:64
  391.1 10.9 %fusion.4 = bf16[16,2,128,256]{3,2,1,0:T(8,128)(2,1)} fusion(f32[16,2,128,256,1]{3,2,4,1,0:T(8,128)S(1)} %fusion.5, bf16[256,14,128,1,1]{0,2,1,4,3:T(8,128)(2,1)S(1)} %bitcast.123, bf16[16,2,14,128,128]{4,2,3,1,0:T(8,128)(2,1)} %fusion), kind=kOutput, calls=%fused_computation.12 | convolution fusion | flops 3760193536 | bytes 21889024 | tf_op jit(solution)/shard_map/frjab,tjb->frat/dot_general | solution.py:66
  402.0 4.1 copy.71
  407.6 99.0 %reduce-scatter.5.cloned.1.call-done = bf16[18,128,256]{2,1,0:T(8,128)(2,1)} async-done(((bf16[288,128,256]{2,1,0:T(8,128)(2,1)}), bf16[18,128,256]{2,1,0:T(8,128)(2,1)}) %reduce-scatter.5.cloned.1.call-update) | async-done | bytes 1179664 | tf_op jit(solution)/shard_map/reduce_scatter | solution.py:88
  506.6 2.4 fusion.26
  509.0 33.7 %reduce-scatter.3.cloned.1.call-done = bf16[512,256]{0,1:T(8,128)(2,1)} async-done(((bf16[4096,256]{0,1:T(8,128)(2,1)}), bf16[512,256]{0,1:T(8,128)(2,1)}) %reduce-scatter.3.cloned.1.call-update) | async-done | bytes 262160 | tf_op jit(solution)/shard_map/reduce_scatter | solution.py:67
  (33 shorter events, 6.7 us)
Async XLA Ops:
  7.2 186.6 %all-gather.3.cloned.1.call-start = ((), (), s32[]{:S(2)}) async-start(), calls=%async_computation.3 | async-start | bytes 2359296 | tf_op jit(solution)/shard_map/all_gather | solution.py:13
  9.0 215.2 %all-gather.5.cloned.1.call-start = ((), (), s32[]{:S(2)}) async-start(), calls=%async_computation.4 | async-start | bytes 10027008 | tf_op jit(solution)/shard_map/all_gather | solution.py:33
  16.9 8.4 %copy-start.6 = (s32[288,1]{0,1:T(1,128)S(1)}, s32[288,1]{0,1:T(1,128)}, u32[]{:S(2)}) copy-start(s32[288,1]{0,1:T(1,128)} %param.9) | copy-start | bytes 3460
  16.9 8.4 %copy-start.7 = (s32[288,1]{0,1:T(1,128)S(1)}, s32[288,1]{0,1:T(1,128)}, u32[]{:S(2)}) copy-start(s32[288,1]{0,1:T(1,128)} %param.10) | copy-start | bytes 3460
  16.9 8.6 %copy-start.5 = (bf16[256,1792]{1,0:T(8,128)(2,1)S(1)}, bf16[256,1792]{1,0:T(8,128)(2,1)}, u32[]{:S(2)}) copy-start(bf16[256,1792]{1,0:T(8,128)(2,1)} %param.11) | copy-start | bytes 2752516
  16.9 160.7 %all-to-all-start = ((bf16[16,18,128,128]{3,2,1,0:T(8,128)(2,1)}), bf16[16,18,128,128]{3,2,1,0:T(8,128)(2,1)}, u32[]{:S(2)}, u32[]{:S(2)}) async-start(bf16[16,18,128,128]{3,2,1,0:T(8,128)(2,1)} %stack.2), calls=%async_computation | async-start | bytes 18874368 | tf_op jit(solution)/shard_map/all_to_all | solution.py:31
  25.2 481.4 %reduce-scatter.5.cloned.1.call-start = ((), (), s32[]{:S(2)}) async-start(), calls=%async_computation.6 | async-start | bytes 20054016 | tf_op jit(solution)/shard_map/reduce_scatter | solution.py:88
  224.3 15.7 %copy-start = (bf16[256,4096]{0,1:T(8,128)(2,1)S(1)}, bf16[256,4096]{0,1:T(8,128)(2,1)}, u32[]{:S(2)}) copy-start(bf16[256,4096]{0,1:T(8,128)(2,1)} %all-gather.3.cloned.1.call-done) | copy-start | bytes 6291460
  240.0 13.6 %copy-start.3 = (bf16[256,1792]{0,1:T(8,128)(2,1)S(1)}, bf16[256,1792]{0,1:T(8,128)(2,1)}, u32[]{:S(2)}) copy-start(bf16[256,1792]{0,1:T(8,128)(2,1)} %copy.68) | copy-start | bytes 2752516
  240.0 13.6 %copy-start.4 = (f32[14,128,256,1,1]{2,1,0,4,3:T(8,128)S(1)}, f32[14,128,256,1,1]{2,1,0,4,3:T(8,128)}, u32[]{:S(2)}) copy-start(f32[14,128,256,1,1]{2,1,0,4,3:T(8,128)} %fusion.6) | copy-start | bytes 5505028
  380.6 1.2 copy-start.1
  380.7 162.0 %reduce-scatter.3.cloned.1.call-start = ((), (), s32[]{:S(2)}) async-start(), calls=%async_computation.5 | async-start | bytes 2359296 | tf_op jit(solution)/shard_map/reduce_scatter | solution.py:67
  391.1 15.1 %copy-start.2 = (bf16[256,1792]{0,1:T(8,128)(2,1)S(1)}, bf16[256,1792]{0,1:T(8,128)(2,1)}, u32[]{:S(2)}) copy-start(bf16[256,1792]{0,1:T(8,128)(2,1)} %get-tuple-element.17) | copy-start | bytes 2752516
Sparse Core Ops, SparseCore 0:
  10.3 27.5 all-gather.2
  40.1 184.1 all-gather.4
  380.8 125.7 reduce-scatter.4
  509.4 33.2 reduce-scatter.2
